TPU v7x, 32 devices: a whole 2x2x4 slice. The times are simulated.
32 devices in a mesh: row: 8 (over z, x), col: 4 (over y, core).
Axes of the slice: x: 2, y: 2, z: 4, core: 2. Of those that a mesh axis runs over, the one named last changes fastest.
Arguments:
- query_sketches: bfloat16 [512, 16384], P('row', 'col'), may hold values from -200 to 200
- fisher_inverse: bfloat16 [16384, 16384], P('row', 'col'), may hold values from -1 to 3, as said below
- index_tiles: bfloat16 [4096, 16384], P('col', 'row'), may hold values from -6 to 6
Outputs:
- scores: float32 [512, 4096], P('row', 'col')
Inputs may be any that keep to these rules, and one draw needn't show every extreme that they name: `fisher_inverse`: symmetric.
All inputs are finite; a program needn't handle non-finite values.
Results may differ from a plain program's by a relative error of at most 0.0029.
Values may be sent and summed in bfloat16 or wider, within the bound.
A program may use at most 64 MiB of HBM per device.

v0:
```python
import jax
import jax.numpy as jnp
from jax import lax
from jax.sharding import PartitionSpec as P


def local(query_sketches, fisher_inverse, index_tiles):
    query_tall = lax.all_gather(query_sketches, "row", axis=0, tiled=True)
    partial_block = lax.dot_general(
        query_tall, fisher_inverse, (((1,), (1,)), ((), ())), preferred_element_type=jnp.float32
    )
    sketch_block = lax.psum(partial_block, "col")
    squares = lax.psum(jnp.sum(sketch_block * sketch_block, axis=1), "row")
    unit_block = (sketch_block / jnp.sqrt(squares + 1e-06)[:, None]).astype(jnp.bfloat16)
    return lax.psum_scatter(
        lax.dot_general(
            unit_block, index_tiles, (((1,), (1,)), ((), ())), preferred_element_type=jnp.float32
        ),
        "row",
        scatter_dimension=0,
        tiled=True,
    )


def solution(mesh):
    placed = (P("row", "col"), P("row", "col"), P("col", "row"))
    return jax.shard_map(
        local, mesh=mesh, in_specs=placed, out_specs=P("row", "col"), check_vma=False
    )
```

profile of v0, /device:TPU:0, one launch (start us, length us, event | category | flops | bytes accessed | tf_op | source)
XLA Modules:
  0.0 287.1 jit_solution(8181149917370606710)
XLA Ops:
  6.5 0.0 all-gather.2.cloned.1.call-start
  6.5 0.7 all-gather.2.cloned.1.call-update
  7.3 0.0 all-reduce.2.cloned.1.call-start
  7.3 78.3 %all-gather.2.cloned.1.call-done = bf16[512,4096]{1,0:T(8,128)(2,1)} async-done(((bf16[64,4096]{1,0:T(8,128)(2,1)}), bf16[512,4096]{1,0:T(8,128)(2,1)}) %all-gather.2.cloned.1.call-update) | async-done | bytes 4194320 | tf_op jit(solution)/shard_map/all_gather | solution.py:8
  85.6 15.0 %fusion.1 = f32[512,2048]{1,0:T(8,128)} fusion(bf16[512,4096]{1,0:T(8,128)(2,1)} %all-gather.2.cloned.1.call-done, bf16[2048,4096]{1,0:T(8,128)(2,1)} %param.4), kind=kOutput, calls=%fused_computation.4 | convolution fusion | flops 8589934592 | bytes 25165824 | tf_op jit(solution)/shard_map/dot_general | solution.py:9
  100.6 0.0 all-reduce.2.cloned.1.call-update
  100.6 0.0 reduce-scatter.2.cloned.1.call-start
  100.7 83.8 %all-reduce.2.cloned.1.call-done = f32[512,2048]{1,0:T(8,128)} async-done(((f32[512,2048]{1,0:T(8,128)}), f32[512,2048]{1,0:T(8,128)}) %all-reduce.2.cloned.1.call-update) | async-done | bytes 4194320 | tf_op jit(solution)/shard_map/psum | solution.py:12
  184.5 2.5 multiply_reduce_fusion
  187.0 21.4 %psum.15 = f32[512]{0:T(512)S(1)} all-reduce(f32[512]{0:T(512)S(1)} %multiply_reduce_fusion), channel_id=1, replica_groups=mesh['row'=8,'col'=4] {'row'}, use_global_device_ids=true, to_apply=%region_2.0 | all-reduce | flops 512 | bytes 4096 | tf_op jit(solution)/shard_map/psum | solution.py:13
  208.4 7.2 %fusion = f32[512,1024]{1,0:T(8,128)} fusion(bf16[1024,2048]{1,0:T(8,128)(2,1)} %param.5, f32[512,2048]{1,0:T(8,128)} %all-reduce.2.cloned.1.call-done, f32[512]{0:T(512)S(1)} %add_sqrt_fusion), kind=kOutput, calls=%fused_computation.2 | convolution fusion | flops 2149580800 | bytes 10487808 | tf_op jit(solution)/shard_map/dot_general | solution.py:16
  215.6 0.0 reduce-scatter.2.cloned.1.call-update
  215.6 65.0 %reduce-scatter.2.cloned.1.call-done = f32[64,1024]{1,0:T(8,128)} async-done(((f32[512,1024]{1,0:T(8,128)}), f32[64,1024]{1,0:T(8,128)}) %reduce-scatter.2.cloned.1.call-update) | async-done | bytes 262160 | tf_op jit(solution)/shard_map/reduce_scatter | solution.py:15
  (1 shorter events, 0.0 us)
Async XLA Ops:
  6.5 79.1 %all-gather.2.cloned.1.call-start = ((), (), s32[]{:S(2)}) async-start(), calls=%async_computation.1 | async-start | bytes 4718592 | tf_op jit(solution)/shard_map/all_gather | solution.py:8
  7.3 177.2 %all-reduce.2.cloned.1.call-start = ((), (), s32[]{:S(2)}) async-start(), calls=%async_computation.2 | async-start | bytes 8388608 | tf_op jit(solution)/shard_map/psum | solution.py:12
  100.6 180.0 %reduce-scatter.2.cloned.1.call-start = ((), (), s32[]{:S(2)}) async-start(), calls=%async_computation.3 | async-start | bytes 2359296 | tf_op jit(solution)/shard_map/reduce_scatter | solution.py:15
Sparse Core Ops, SparseCore 0:
  9.5 76.0 all-gather.1
  100.7 83.7 all-reduce.1
  215.7 64.8 reduce-scatter.1
where the time goes:
time: 287 us
  waiting for transfers between devices  228 us (79%)
  matrix products  22.1 us (8%)
  blocking collectives  21.4 us (7%)
  between operations  13.1 us (5%)
    psum x1, waiting for transfers between devices, local(): sketch_block = lax.psum(partial_block, 'col')  83.8 us
    all_gather x1, waiting for transfers between devices, local(): query_tall = lax.all_gather(query_sketches, 'row', axis=0, tiled=True)  78.3 us
    reduce_scatter x1, waiting for transfers between devices, local(): lax.psum_scatter(lax.dot_general(unit_block, index_tiles, (((1,), (1,)),...  65 us
    psum x1, blocking collectives, local(): squares = lax.psum(jnp.sum(sketch_block * sketch_block, axis=1), 'row')  21.4 us
    dot_general x1, matrix products, local(): lax.dot_general(query_tall, fisher_inverse, (((1,), (1,)), ((), ())), pre...  15 us
    dot_general x1, matrix products, local(): lax.dot_general(unit_block, index_tiles, (((1,), (1,)), ((), ())), prefer...  7.18 us
  transfers between devices with their start and end apart: 3, of which 3 were waited for; matrix products, arithmetic and copies ran while one was open for 0% of the time, Pallas kernels for 0%

commit v1 on v0

v1 whole, which is shorter than its diff:
```python
import functools

import jax
import jax.numpy as jnp
from jax import lax
from jax.experimental import pallas as pl
from jax.experimental.pallas import tpu as pltpu
from jax.sharding import PartitionSpec as P

NT = (((1,), (1,)), ((), ()))
Y_DTYPE = jnp.float32


def nt_dot(a, b):
    return lax.dot_general(a, b, NT, preferred_element_type=jnp.float32)


def kernel(
    line, groups, q_hbm, f_hbm, i_hbm, out_ref,
    qbuf, fbuf, ibuf, part, cbuf, half_sum, y_src, ybuf, full, keep, sx_src, sx_dst,
    sz_src, sz_dst, sq_src, sq_dst, sq_col, acc,
    load_sem, g_recv, up_send, dn_send, x_send, c1_send, c1_recv, y_send, y_recv,
    c2_send, c2_recv, sx_send, sx_recv, sz_send, sz_recv, sq_send, sq_recv,
):
    r, c = lax.axis_index("row"), lax.axis_index("col")
    z, x = r // 2, r % 2
    y, core = c // 2, c % 2
    qb, fr = qbuf.shape[2], fbuf.shape[0]
    pair, hf = 2 * qb, fr // 2
    tile = min(256, hf)
    n_row, n_col = 2 * line, 2 * groups

    load_q = pltpu.make_async_copy(q_hbm, qbuf.at[z, x], load_sem.at[0])
    load_f = pltpu.make_async_copy(f_hbm, fbuf, load_sem.at[1])
    load_i = pltpu.make_async_copy(i_hbm, ibuf, load_sem.at[2])
    load_q.start()
    load_f.start()
    load_i.start()

    def remote(src, dst, send, recv, row, col):
        return pltpu.make_async_remote_copy(
            src_ref=src, dst_ref=dst, send_sem=send, recv_sem=recv,
            device_id=(row, col), device_id_type=pl.DeviceIdType.MESH,
        )

    barrier = pltpu.get_barrier_semaphore()
    sibling = c + 1 - 2 * core
    for d in range(1, n_row):
        pl.semaphore_signal(
            barrier, inc=1, device_id=(lax.rem(r + d, n_row), c), device_id_type=pl.DeviceIdType.MESH
        )
    pl.semaphore_signal(barrier, inc=1, device_id=(r, sibling), device_id_type=pl.DeviceIdType.MESH)
    for g in range(1, groups):
        pl.semaphore_signal(
            barrier, inc=1, device_id=(r, lax.rem(c + 2 * g, n_col)), device_id_type=pl.DeviceIdType.MESH
        )
    pl.semaphore_wait(barrier, n_row - 1 + groups)

    near = jnp.minimum(z, line - 1 - z)

    def order(j):
        step = (j + 1) // 2
        close = z + step * (2 * (j % 2) - 1)
        far = jnp.where(z < line - 1 - z, j, line - 1 - j)
        return jnp.where(j <= 2 * near, close, far)

    def up_copy(zb):
        return remote(qbuf.at[zb, x], qbuf.at[zb, x], up_send.at[zb], g_recv.at[zb, x], r + 2, c)

    def dn_copy(zb):
        return remote(qbuf.at[zb, x], qbuf.at[zb, x], dn_send.at[zb], g_recv.at[zb, x], r - 2, c)

    def x_copy(zb):
        return remote(qbuf.at[zb, x], qbuf.at[zb, x], x_send.at[zb], g_recv.at[zb, x], r + 1 - 2 * x, c)

    def c1_copy(j):
        return remote(part.at[j, 1 - core], cbuf.at[j], c1_send.at[j], c1_recv.at[j], r, sibling)

    def y_copy(j, g):
        return remote(
            y_src.at[j], ybuf.at[g - 1, j], y_send.at[g - 1, j], y_recv.at[g - 1, j],
            r, lax.rem(c + 2 * g, n_col),
        )

    def c2_copy(j):
        return remote(full.at[j, core], full.at[j, core], c2_send.at[j], c2_recv.at[j], r, sibling)

    def sx_copy(j):
        return remote(sx_src.at[j], sx_dst.at[j], sx_send.at[j], sx_recv.at[j], r + 1 - 2 * x, c)

    def sz_copy(zb):
        return remote(sz_src.at[zb], sz_dst.at[z], sz_send.at[zb], sz_recv.at[z], 2 * zb + x, c)

    def sq_copy(zb, xb):
        return remote(sq_src.at[zb], sq_dst.at[z, x], sq_send.at[zb, xb], sq_recv.at[z, x], 2 * zb + xb, c)

    def forward(zb):
        x_copy(zb).start()

        @pl.when((zb <= z) & (z < line - 1))
        def _():
            up_copy(zb).start()

        @pl.when((zb >= z) & (z > 0))
        def _():
            dn_copy(zb).start()

    load_q.wait()
    forward(z)
    load_f.wait()
    load_i.wait()

    def wait_block(zb, xb):
        remote(qbuf.at[zb, xb], qbuf.at[zb, xb], x_send.at[zb], g_recv.at[zb, xb], r, c).wait_recv()

    def body(t, carry):
        @pl.when(t + 1 < line)
        def _():
            zb = order(t + 1)
            wait_block(zb, x)
            forward(zb)

        @pl.when(t < line)
        def _():
            zb = order(t)
            wait_block(zb, 1 - x)
            for h in range(2):
                @pl.loop(0, hf // tile)
                def _(n):
                    at = pl.multiple_of(n * tile, tile)
                    lhs = qbuf[zb].reshape(pair, qbuf.shape[3])
                    part[t, h, :, pl.ds(at, tile)] = nt_dot(lhs, fbuf[pl.ds(h * hf + at, tile), :])
            c1_copy(t).start()

        @pl.when((t >= 1) & (t <= line))
        def _():
            j = t - 1
            total = half_sum[j]
            for g in range(1, groups):
                y_copy(j, g).wait_recv()
                total += ybuf[g - 1, j].astype(jnp.float32)
            full[j, core] = total
            c2_copy(j).start()

        @pl.when(t < line)
        def _():
            c1_copy(t).wait_recv()
            total = part[t, core] + cbuf[t]
            half_sum[t] = total
            y_src[t] = total.astype(y_src.dtype)
            for g in range(1, groups):
                y_copy(t, g).start()

        @pl.when((t >= 1) & (t <= line))
        def _():
            j = t - 1
            zb = order(j)
            remote(
                full.at[j, 1 - core], full.at[j, 1 - core], c2_send.at[j], c2_recv.at[j], r, sibling
            ).wait_recv()
            square = jnp.zeros((8, pair), jnp.float32)
            score = jnp.zeros((pair, ibuf.shape[0]), jnp.float32)
            for h in range(2):
                p = full[j, h]
                square += lax.dot_general(
                    jnp.ones((8, hf), jnp.float32), p * p, NT,
                    preferred_element_type=jnp.float32, precision=lax.Precision.HIGHEST,
                )
                high = p.astype(jnp.bfloat16)
                low = (p - high.astype(jnp.float32)).astype(jnp.bfloat16)
                w = ibuf[:, h * hf:(h + 1) * hf]
                score += nt_dot(jnp.concatenate([high, low], axis=0), w).reshape(2, pair, -1).sum(0)
            sq_src[zb] = square
            keep[j] = score.reshape(2, qb, -1)
            sx_src[j] = keep[j, 1 - x].astype(jnp.bfloat16)
            sx_copy(j).start()
            sq_copy(zb, 1 - x).start()

            @pl.when(zb != z)
            def _():
                sq_copy(zb, x).start()

        @pl.when(t >= 2)
        def _():
            j = t - 2
            zb = order(j)
            sx_copy(j).wait_recv()
            total = keep[j, x] + sx_dst[j].astype(jnp.float32)

            @pl.when(zb == z)
            def _():
                acc[...] = total

            @pl.when(zb != z)
            def _():
                sz_src[zb] = total.astype(jnp.bfloat16)
                sz_copy(zb).start()

        return carry

    lax.fori_loop(0, line + 2, body, 0)

    def gather_squares(zb, carry):
        def one(xb):
            remote(
                sq_src.at[zb], sq_dst.at[zb, xb], sq_send.at[zb, xb], sq_recv.at[zb, xb], r, c
            ).wait_recv()
            return sq_dst[zb, xb]

        sq_col[...] += one(1 - x)

        @pl.when(zb != z)
        def _():
            sq_col[...] += one(x)
            remote(sz_src.at[zb], sz_dst.at[zb], sz_send.at[zb], sz_recv.at[zb], r, c).wait_recv()
            acc[...] += sz_dst[zb].astype(jnp.float32)

        return carry

    sq_col[...] = sq_src[z]
    lax.fori_loop(0, line, gather_squares, 0)
    scale = lax.rsqrt(sq_col[...] + 1e-06)
    column = jnp.transpose(scale)[:, :1]
    mine = jnp.where(x == 0, column[:qb], column[qb:])
    out_ref[...] = acc[...] * mine

    def drain(j, carry):
        x_copy(j).wait_send()

        @pl.when((j <= z) & (z < line - 1))
        def _():
            up_copy(j).wait_send()

        @pl.when((j >= z) & (z > 0))
        def _():
            dn_copy(j).wait_send()

        c1_copy(j).wait_send()
        for g in range(1, groups):
            y_copy(j, g).wait_send()
        c2_copy(j).wait_send()
        sx_copy(j).wait_send()
        sq_copy(j, 1 - x).wait_send()

        @pl.when(j != z)
        def _():
            sq_copy(j, x).wait_send()
            sz_copy(j).wait_send()

        return carry

    lax.fori_loop(0, line, drain, 0)


def local(n_row, n_col, q, f, i):
    line, groups = n_row // 2, n_col // 2
    qb, fc = q.shape
    fr, ib = f.shape[0], i.shape[0]
    pair, hf = 2 * qb, fr // 2
    dma = pltpu.SemaphoreType.DMA
    vm = pltpu.VMEM
    f32, bf16 = jnp.float32, jnp.bfloat16
    peers = max(groups - 1, 1)
    return pl.pallas_call(
        functools.partial(kernel, line, groups),
        out_shape=jax.ShapeDtypeStruct((qb, ib), f32),
        in_specs=[pl.BlockSpec(memory_space=pl.ANY)] * 3,
        out_specs=pl.BlockSpec(memory_space=pltpu.VMEM),
        scratch_shapes=[
            vm((line, 2, qb, fc), bf16),
            vm((fr, fc), bf16),
            vm((ib, fr), bf16),
            vm((line, 2, pair, hf), f32),
            vm((line, pair, hf), f32),
            vm((line, pair, hf), f32),
            vm((line, pair, hf), Y_DTYPE),
            vm((peers, line, pair, hf), Y_DTYPE),
            vm((line, 2, pair, hf), f32),
            vm((line, 2, qb, ib), f32),
            vm((line, qb, ib), bf16),
            vm((line, qb, ib), bf16),
            vm((line, qb, ib), bf16),
            vm((line, qb, ib), bf16),
            vm((line, 8, pair), f32),
            vm((line, 2, 8, pair), f32),
            vm((8, pair), f32),
            vm((qb, ib), f32),
            dma((3,)),
            dma((line, 2)),
            dma((line,)), dma((line,)), dma((line,)),
            dma((line,)), dma((line,)),
            dma((peers, line)), dma((peers, line)),
            dma((line,)), dma((line,)),
            dma((line,)), dma((line,)),
            dma((line,)), dma((line,)),
            dma((line, 2)), dma((line, 2)),
        ],
        compiler_params=pltpu.CompilerParams(
            collective_id=0, has_side_effects=True, vmem_limit_bytes=60 * 1024 * 1024
        ),
        cost_estimate=pl.CostEstimate(
            flops=2 * n_row * qb * fr * (fc + 2 * ib),
            bytes_accessed=2 * (fr * fc + ib * fr + qb * fc) + 4 * qb * ib,
            transcendentals=0,
        ),
    )(q, f, i)


def solution(mesh):
    placed = (P("row", "col"), P("row", "col"), P("col", "row"))
    return jax.shard_map(
        functools.partial(local, mesh.shape["row"], mesh.shape["col"]),
        mesh=mesh, in_specs=placed, out_specs=P("row", "col"), check_vma=False,
    )
```

time: 287 us -> 108 us (0.38)
  waiting for transfers between devices: 228 us -> 0 us
  Pallas kernels: 0 us -> 106 us
  matrix products: 22.1 us -> 0 us
  blocking collectives: 21.4 us -> 0 us
  between operations: 13.1 us -> 0.01 us
    pallas_call x0 -> x1, Pallas kernels: none -> 106 us  [local(): pl.pallas_call(functools.partial(kernel, line, groups), out_shape=jax.Sha...]
    psum x1 -> x0, waiting for transfers between devices: 83.8 us -> none  [local(): sketch_block = lax.psum(partial_block, 'col')]
    all_gather x1 -> x0, waiting for transfers between devices: 78.3 us -> none  [local(): query_tall = lax.all_gather(query_sketches, 'row', axis=0, tiled=True)]
    reduce_scatter x1 -> x0, waiting for transfers between devices: 65 us -> none  [local(): lax.psum_scatter(lax.dot_general(unit_block, index_tiles, (((1,), (1,)),...]
    dot_general x2 -> x0, matrix products: 22.1 us -> none  [the longest x1 15 us: local(): lax.dot_general(query_tall, fisher_inverse, (((1,), (1,)), ((), ())), pre...]
    psum x1 -> x0, blocking collectives: 21.4 us -> none  [local(): squares = lax.psum(jnp.sum(sketch_block * sketch_block, axis=1), 'row')]
  transfers between devices with their start and end apart: 3 -> 0, of which waited for: 3 -> 0; matrix products, arithmetic and copies ran while one was open for 0% -> 0% of each run, Pallas kernels for 0% -> 0%
where the time goes in v1:
time: 108 us
  Pallas kernels  106 us (98%)
  local copies, waits for them, and re-layouts  1.67 us (2%)
    pallas_call x1, Pallas kernels, local(): pl.pallas_call(functools.partial(kernel, line, groups), out_shape=jax.Sha...  106 us

profile of v1, /device:TPU:0, one launch (start us, length us, event | category | flops | bytes accessed | tf_op | source)
XLA Modules:
  0.0 107.9 jit_solution(11903354923564402175)
XLA Ops:
  0.0 106.2 %shard_map.37 = f32[64,1024]{1,0:T(8,128)} custom-call(bf16[64,4096]{1,0:T(8,128)(2,1)} %q_hbm.1, bf16[2048,4096]{1,0:T(8,128)(2,1)} %f_hbm.1, bf16[1024,2048]{1,0:T(8,128)(2,1)} %i_hbm.1), custom_call_target="tpu_custom_call" | custom-call | flops 12884901888 | bytes 21757952 | tf_op jit(solution)/shard_map/pallas_call | solution.py:264
  106.2 1.7 %copy.5 = f32[64,1024]{1,0:T(8,128)} copy(f32[64,1024]{1,0:T(8,128)} %shard_map.37) | data formatting | bytes 524288

commit v2 on v1

--- a/solution.py
+++ b/solution.py
@@ -8,8 +8,6 @@
 from jax.sharding import PartitionSpec as P
 
 NT = (((1,), (1,)), ((), ()))
-Y_DTYPE = jnp.float32
-
 
 def nt_dot(a, b):
     return lax.dot_general(a, b, NT, preferred_element_type=jnp.float32)
@@ -17,7 +15,7 @@
 
 def kernel(
     line, groups, q_hbm, f_hbm, i_hbm, out_ref,
-    qbuf, fbuf, ibuf, part, cbuf, half_sum, y_src, ybuf, full, keep, sx_src, sx_dst,
+    qbuf, fbuf, ibuf, part, cbuf, half_sum, y_src, ybuf, ywide, full, keep, sx_src, sx_dst,
     sz_src, sz_dst, sq_src, sq_dst, sq_col, acc,
     load_sem, g_recv, up_send, dn_send, x_send, c1_send, c1_recv, y_send, y_recv,
     c2_send, c2_recv, sx_send, sx_recv, sz_send, sz_recv, sq_send, sq_recv,
@@ -82,6 +80,14 @@
             r, lax.rem(c + 2 * g, n_col),
         )
 
+    def y_wide_copy(j, g):
+        return remote(
+            half_sum.at[j], ywide.at[g - 1, j], y_send.at[g - 1, j], y_recv.at[g - 1, j],
+            r, lax.rem(c + 2 * g, n_col),
+        )
+
+    wide = line - line // 2
+
     def c2_copy(j):
         return remote(full.at[j, core], full.at[j, core], c2_send.at[j], c2_recv.at[j], r, sibling)
 
@@ -107,18 +113,23 @@
 
     load_q.wait()
     forward(z)
+
+    def wait_block(zb, xb):
+        remote(qbuf.at[zb, xb], qbuf.at[zb, xb], x_send.at[zb], g_recv.at[zb, xb], r, c).wait_recv()
+
+    def take(zb):
+        wait_block(zb, x)
+        forward(zb)
+
+    if line > 1:
+        take(order(1))
     load_f.wait()
     load_i.wait()
 
-    def wait_block(zb, xb):
-        remote(qbuf.at[zb, xb], qbuf.at[zb, xb], x_send.at[zb], g_recv.at[zb, xb], r, c).wait_recv()
-
     def body(t, carry):
-        @pl.when(t + 1 < line)
-        def _():
-            zb = order(t + 1)
-            wait_block(zb, x)
-            forward(zb)
+        @pl.when(t + 2 < line)
+        def _():
+            take(order(t + 2))
 
         @pl.when(t < line)
         def _():
@@ -132,28 +143,9 @@
                     part[t, h, :, pl.ds(at, tile)] = nt_dot(lhs, fbuf[pl.ds(h * hf + at, tile), :])
             c1_copy(t).start()
 
-        @pl.when((t >= 1) & (t <= line))
-        def _():
-            j = t - 1
-            total = half_sum[j]
-            for g in range(1, groups):
-                y_copy(j, g).wait_recv()
-                total += ybuf[g - 1, j].astype(jnp.float32)
-            full[j, core] = total
-            c2_copy(j).start()
-
-        @pl.when(t < line)
-        def _():
-            c1_copy(t).wait_recv()
-            total = part[t, core] + cbuf[t]
-            half_sum[t] = total
-            y_src[t] = total.astype(y_src.dtype)
-            for g in range(1, groups):
-                y_copy(t, g).start()
-
-        @pl.when((t >= 1) & (t <= line))
-        def _():
-            j = t - 1
+        @pl.when((t >= 2) & (t <= line + 1))
+        def _():
+            j = t - 2
             zb = order(j)
             remote(
                 full.at[j, 1 - core], full.at[j, 1 - core], c2_send.at[j], c2_recv.at[j], r, sibling
@@ -180,9 +172,48 @@
             def _():
                 sq_copy(zb, x).start()
 
-        @pl.when(t >= 2)
-        def _():
-            j = t - 2
+        @pl.when(t < line)
+        def _():
+            c1_copy(t).wait_recv()
+            total = part[t, core] + cbuf[t]
+            half_sum[t] = total
+
+            @pl.when(t < wide)
+            def _():
+                for g in range(1, groups):
+                    y_wide_copy(t, g).start()
+
+            @pl.when(t >= wide)
+            def _():
+                y_src[t] = total.astype(y_src.dtype)
+                for g in range(1, groups):
+                    y_copy(t, g).start()
+
+        @pl.when((t >= 1) & (t <= line))
+        def _():
+            j = t - 1
+
+            @pl.when(j < wide)
+            def _():
+                total = half_sum[j]
+                for g in range(1, groups):
+                    y_wide_copy(j, g).wait_recv()
+                    total += ywide[g - 1, j]
+                full[j, core] = total
+
+            @pl.when(j >= wide)
+            def _():
+                total = half_sum[j]
+                for g in range(1, groups):
+                    y_copy(j, g).wait_recv()
+                    total += ybuf[g - 1, j].astype(jnp.float32)
+                full[j, core] = total
+
+            c2_copy(j).start()
+
+        @pl.when(t >= 3)
+        def _():
+            j = t - 3
             zb = order(j)
             sx_copy(j).wait_recv()
             total = keep[j, x] + sx_dst[j].astype(jnp.float32)
@@ -198,7 +229,7 @@
 
         return carry
 
-    lax.fori_loop(0, line + 2, body, 0)
+    lax.fori_loop(0, line + 3, body, 0)
 
     def gather_squares(zb, carry):
         def one(xb):
@@ -236,8 +267,17 @@
             dn_copy(j).wait_send()
 
         c1_copy(j).wait_send()
-        for g in range(1, groups):
-            y_copy(j, g).wait_send()
+
+        @pl.when(j < wide)
+        def _():
+            for g in range(1, groups):
+                y_wide_copy(j, g).wait_send()
+
+        @pl.when(j >= wide)
+        def _():
+            for g in range(1, groups):
+                y_copy(j, g).wait_send()
+
         c2_copy(j).wait_send()
         sx_copy(j).wait_send()
         sq_copy(j, 1 - x).wait_send()
@@ -273,8 +313,9 @@
             vm((line, 2, pair, hf), f32),
             vm((line, pair, hf), f32),
             vm((line, pair, hf), f32),
-            vm((line, pair, hf), Y_DTYPE),
-            vm((peers, line, pair, hf), Y_DTYPE),
+            vm((line, pair, hf), bf16),
+            vm((peers, line, pair, hf), bf16),
+            vm((peers, line, pair, hf), f32),
             vm((line, 2, pair, hf), f32),
             vm((line, 2, qb, ib), f32),
             vm((line, qb, ib), bf16),

time: 108 us -> 96.5 us (0.89)
  Pallas kernels: 106 us -> 94.7 us
    pallas_call x1, Pallas kernels: 106 us -> 94.7 us  [local(): pl.pallas_call(functools.partial(kernel, line, groups), out_shape=jax.Sha...]
where the time goes in v2:
time: 96.5 us; the launch traced here: 96.4 us
  Pallas kernels  94.7 us (98%)
  local copies, waits for them, and re-layouts  1.67 us (2%)
    pallas_call x1, Pallas kernels, local(): pl.pallas_call(functools.partial(kernel, line, groups), out_shape=jax.Sha...  94.7 us

profile of v2, /device:TPU:0, one launch (start us, length us, event | category | flops | bytes accessed | tf_op | source)
XLA Modules:
  0.0 96.4 jit_solution(11226549822175862590)
XLA Ops:
  0.0 94.7 %shard_map.37 = f32[64,1024]{1,0:T(8,128)} custom-call(bf16[64,4096]{1,0:T(8,128)(2,1)} %q_hbm.1, bf16[2048,4096]{1,0:T(8,128)(2,1)} %f_hbm.1, bf16[1024,2048]{1,0:T(8,128)(2,1)} %i_hbm.1), custom_call_target="tpu_custom_call" | custom-call | flops 12884901888 | bytes 21757952 | tf_op jit(solution)/shard_map/pallas_call | solution.py:304
  94.7 1.7 %copy.5 = f32[64,1024]{1,0:T(8,128)} copy(f32[64,1024]{1,0:T(8,128)} %shard_map.37) | data formatting | bytes 524288

commit v3 on v2

--- a/solution.py
+++ b/solution.py
@@ -25,7 +25,7 @@
     y, core = c // 2, c % 2
     qb, fr = qbuf.shape[2], fbuf.shape[0]
     pair, hf = 2 * qb, fr // 2
-    tile = min(256, hf)
+    tile = min(512, hf)
     n_row, n_col = 2 * line, 2 * groups
 
     load_q = pltpu.make_async_copy(q_hbm, qbuf.at[z, x], load_sem.at[0])
@@ -135,24 +135,28 @@
         def _():
             zb = order(t)
             wait_block(zb, 1 - x)
-            for h in range(2):
+            for h in (1 - core, core):
                 @pl.loop(0, hf // tile)
                 def _(n):
                     at = pl.multiple_of(n * tile, tile)
-                    lhs = qbuf[zb].reshape(pair, qbuf.shape[3])
-                    part[t, h, :, pl.ds(at, tile)] = nt_dot(lhs, fbuf[pl.ds(h * hf + at, tile), :])
-            c1_copy(t).start()
+                    rhs = qbuf[zb].reshape(pair, qbuf.shape[3])
+                    rows = pl.ds(pl.multiple_of(h * hf + at, tile), tile)
+                    part[t, h, :, pl.ds(at, tile)] = nt_dot(fbuf[rows, :], rhs).T
+
+                if h is not core:
+                    c1_copy(t).start()
 
         @pl.when((t >= 2) & (t <= line + 1))
         def _():
             j = t - 2
             zb = order(j)
-            remote(
-                full.at[j, 1 - core], full.at[j, 1 - core], c2_send.at[j], c2_recv.at[j], r, sibling
-            ).wait_recv()
             square = jnp.zeros((8, pair), jnp.float32)
             score = jnp.zeros((pair, ibuf.shape[0]), jnp.float32)
-            for h in range(2):
+            for h in (core, 1 - core):
+                if h is not core:
+                    remote(
+                        full.at[j, h], full.at[j, h], c2_send.at[j], c2_recv.at[j], r, sibling
+                    ).wait_recv()
                 p = full[j, h]
                 square += lax.dot_general(
                     jnp.ones((8, hf), jnp.float32), p * p, NT,
@@ -160,7 +164,7 @@
                 )
                 high = p.astype(jnp.bfloat16)
                 low = (p - high.astype(jnp.float32)).astype(jnp.bfloat16)
-                w = ibuf[:, h * hf:(h + 1) * hf]
+                w = ibuf[:, pl.ds(pl.multiple_of(h * hf, hf), hf)]
                 score += nt_dot(jnp.concatenate([high, low], axis=0), w).reshape(2, pair, -1).sum(0)
             sq_src[zb] = square
             keep[j] = score.reshape(2, qb, -1)

time: 96.5 us -> 92.9 us (0.963)
  Pallas kernels: 94.7 us -> 91.1 us
    pallas_call x1, Pallas kernels: 94.7 us -> 91.1 us  [local(): pl.pallas_call(functools.partial(kernel, line, groups), out_shape=jax.Sha...]
where the time goes in v3:
time: 92.9 us; the launch traced here: 92.8 us
  Pallas kernels  91.1 us (98%)
  local copies, waits for them, and re-layouts  1.67 us (2%)
    pallas_call x1, Pallas kernels, local(): pl.pallas_call(functools.partial(kernel, line, groups), out_shape=jax.Sha...  91.1 us

profile of v3, /device:TPU:0, one launch (start us, length us, event | category | flops | bytes accessed | tf_op | source)
XLA Modules:
  0.0 92.8 jit_solution(6986805934449809115)
XLA Ops:
  0.0 91.1 %shard_map.37 = f32[64,1024]{1,0:T(8,128)} custom-call(bf16[64,4096]{1,0:T(8,128)(2,1)} %q_hbm.1, bf16[2048,4096]{1,0:T(8,128)(2,1)} %f_hbm.1, bf16[1024,2048]{1,0:T(8,128)(2,1)} %i_hbm.1), custom_call_target="tpu_custom_call" | custom-call | flops 12884901888 | bytes 21757952 | tf_op jit(solution)/shard_map/pallas_call | solution.py:308
  91.1 1.7 %copy.5 = f32[64,1024]{1,0:T(8,128)} copy(f32[64,1024]{1,0:T(8,128)} %shard_map.37) | data formatting | bytes 524288
